TPU v7x, 32 devices: a whole 2x2x4 slice. The times are simulated.
32 devices in a mesh: half: 2 (over core), cls: 4 (over z), vol: 4 (over y, x).
Axes of the slice: x: 2, y: 2, z: 4, core: 2. Of those that a mesh axis runs over, the one named last changes fastest.
Arguments:
- images: bfloat16 [1024, 16384], P(('half', 'cls'), 'vol')
- groups: int32 [1024, 1], P(('half', 'cls')), may hold values from 0 to 3; in each aligned block of 128 rows (0 to 127, 128 to 255, ...) at most 64 rows name the same one
- references: bfloat16 [128, 16384], P('cls', 'vol'), may hold values from -0.046875 to 0.046875
- interp_index: int32 [128, 16384], P('cls', 'vol'), may hold values from 0 to 2047
- shell_index: int32 [4, 262144], P('vol', ('half', 'cls')), may hold values from 0 to 127
Outputs:
- volume: float32 [4, 262144], P('vol', ('half', 'cls'))
- shell_fsc: float32 [128], replicated
Inputs may be any that keep to these rules, and one draw needn't show every extreme that they name: `groups`: within each aligned block of 128 particles no group appears more than 64 times, a bound that some block reaches.
All inputs are finite; a program needn't handle non-finite values.
Results may differ from a plain program's by a relative error of at most 0.00041.
Values may be sent and summed in bfloat16 or wider, within the bound.
A program may use at most 64 MiB of HBM per device.

v0:
```python
import jax
import jax.numpy as jnp
from jax import lax
from jax.sharding import PartitionSpec as P

IMG = 128
SHIFTS = 5
NSHELL = 128
PLANES = 4
VBOX = 256
VOXS = 262144


EPS_W = 1e-05
EPS_F = 1e-06


def partner(shard, axis, apart):
    return lax.ppermute(shard, axis, [(i, i ^ 1 << apart) for i in range(lax.axis_size(axis))])


def shards(images, groups, references, interp_index, shell_index):
    n_cls = lax.axis_size("cls")
    n_vol = lax.axis_size("vol")
    n_half = lax.axis_size("half")
    part_count, pix_quarter = images.shape
    class_count = references.shape[0]
    capacity = max(2 * part_count // n_cls, 4)
    slot_count = n_cls * capacity
    owner_ids = groups[:, 0]
    matches = (owner_ids[:, None] == jnp.arange(n_cls, dtype=jnp.int32)[None, :]).astype(jnp.int32)
    order_in = jnp.sum(jnp.cumsum(matches, axis=0) * matches, axis=1) - 1
    slot_ids = owner_ids * capacity + order_in
    slot_hits = slot_ids[None, :] == jnp.arange(slot_count, dtype=jnp.int32)[:, None]
    source_ids = jnp.sum(
        jnp.where(slot_hits, jnp.arange(part_count, dtype=jnp.int32)[None, :], 0), axis=1
    )
    filled = jnp.any(slot_hits, axis=1)
    outgoing = jnp.where(
        filled[:, None], jnp.take(images, source_ids, axis=0), jnp.zeros((), jnp.bfloat16)
    )
    arrived = lax.all_to_all(
        outgoing.reshape(n_cls, capacity, pix_quarter),
        "cls",
        split_axis=0,
        concat_axis=0,
        tiled=True,
    )
    arrived = arrived.reshape(slot_count, pix_quarter)
    quarter_rows = pix_quarter // IMG
    shaped_refs = references.reshape(class_count, quarter_rows, IMG)
    rolled_refs = jnp.concatenate(
        [
            jnp.roll(shaped_refs, -(shift_id - SHIFTS // 2), axis=2).reshape(
                class_count, pix_quarter
            )
            for shift_id in range(SHIFTS)
        ],
        axis=0,
    )
    partial_scores = lax.dot_general(
        arrived, rolled_refs, (((1,), (1,)), ((), ())), preferred_element_type=jnp.float32
    )
    partial_scores = partial_scores.reshape(slot_count, SHIFTS, class_count)
    scores = lax.psum(partial_scores, "vol")
    squares = scores * scores
    mean_square = jnp.mean(squares, axis=(1, 2), keepdims=True)
    weights = (squares / (mean_square + EPS_W)).astype(jnp.bfloat16)
    weighted = lax.dot_general(
        weights.reshape(slot_count, SHIFTS * class_count),
        arrived,
        (((0,), (0,)), ((), ())),
        preferred_element_type=jnp.float32,
    )
    weighted = weighted.reshape(SHIFTS, class_count, quarter_rows, IMG)
    aligned = jnp.roll(weighted[0], -(SHIFTS // 2), axis=2)
    for shift_id in range(1, SHIFTS):
        aligned = aligned + jnp.roll(weighted[shift_id], shift_id - SHIFTS // 2, axis=2)
    column_ids = jnp.arange(pix_quarter, dtype=jnp.int32) % IMG
    placed = interp_index + 2 * VBOX * PLANES * column_ids[None, :]
    slab_part = jax.ops.segment_sum(aligned.reshape(-1), placed.reshape(-1), num_segments=VOXS)
    piece_len = VOXS // (n_half * n_cls)
    slab_part = jnp.transpose(slab_part.reshape(n_half, n_cls, piece_len), (1, 0, 2)).reshape(-1)
    block_len = VOXS // n_cls
    slab_full = lax.psum(slab_part, "cls")
    own_block = lax.dynamic_slice_in_dim(slab_full, lax.axis_index("cls") * block_len, block_len)
    half_id = lax.axis_index("half")
    own_piece = lax.dynamic_slice_in_dim(own_block, half_id * piece_len, piece_len)
    other_piece = lax.dynamic_slice_in_dim(own_block, (1 - half_id) * piece_len, piece_len)
    mirror_piece = partner(other_piece, "half", 0)
    first = jnp.where(half_id == 0, own_piece, mirror_piece)
    second = jnp.where(half_id == 0, mirror_piece, own_piece)
    shell_hot = (shell_index[0][:, None] == jnp.arange(NSHELL, dtype=jnp.int32)[None, :]).astype(
        jnp.float32
    )
    stats = jnp.stack([first * first, second * second, first * second])
    shell_terms = jnp.dot(stats, shell_hot, precision=lax.Precision.HIGHEST)
    shell_sums = lax.psum(shell_terms, ("half", "cls", "vol"))
    shell_fsc = shell_sums[2] / (jnp.sqrt(shell_sums[0]) * jnp.sqrt(shell_sums[1]) + EPS_F)
    mean_sq = (jnp.sum(shell_sums[0]) + jnp.sum(shell_sums[1]) + 2.0 * jnp.sum(shell_sums[2])) / (
        4.0 * n_vol * VOXS
    )
    filter_vox = jnp.dot(shell_hot, shell_fsc, precision=lax.Precision.HIGHEST)
    volume = filter_vox * (0.5 * (first + second)) / jnp.sqrt(mean_sq + EPS_F)
    return (volume[None, :], shell_fsc)


def solution(mesh):
    placed = (
        P(("half", "cls"), "vol"),
        P(("half", "cls"), None),
        P("cls", "vol"),
        P("cls", "vol"),
        P("vol", ("half", "cls")),
    )
    return jax.shard_map(
        shards,
        mesh=mesh,
        in_specs=placed,
        out_specs=(P("vol", ("half", "cls")), P()),
        check_vma=False,
    )
```

profile of v0, /device:TPU:0, one launch (start us, length us, event | category | flops | bytes accessed | tf_op | source)
XLA Modules:
  0.0 927.5 jit_solution(14313329209926463241)
XLA Ops:
  7.2 0.8 fusion.12
  8.2 0.8 select_reduce_fusion.1
  9.0 0.7 add_add_fusion.1
  10.1 1.8 gather_fusion
  12.0 1.7 select_select_fusion
  13.7 6.4 all-to-all-start
  21.1 0.8 bitcast_dynamic-update-slice_fusion.3
  22.2 0.8 bitcast_dynamic-update-slice_fusion.2
  23.0 0.7 constant_dynamic-update-slice_fusion
  23.7 0.8 bitcast_dynamic-update-slice_fusion.1
  24.5 0.8 bitcast_dynamic-update-slice_fusion
  25.3 43.0 %all-to-all-done = bf16[4,64,4096]{2,1,0:T(8,128)(2,1)S(1)} async-done(((bf16[4,64,4096]{2,1,0:T(8,128)(2,1)}), bf16[4,64,4096]{2,1,0:T(8,128)(2,1)S(1)}, u32[]{:S(2)}, u32[]{:S(2)}) %all-to-all-start) | async-done | bytes 2097184 | tf_op jit(solution)/shard_map/all_to_all | solution.py:42
  68.3 2.8 fusion.25
  71.2 1.1 add_bitcast_fusion
  72.3 0.9 copy.9
  73.2 39.5 %all-reduce.3.cloned.1.call-done = f32[256,5,32]{0,2,1:T(8,128)} async-done(((f32[256,5,32]{0,2,1:T(8,128)}), f32[256,5,32]{0,2,1:T(8,128)}) %all-reduce.3.cloned.1.call-update) | async-done | bytes 163856 | tf_op jit(solution)/shard_map/psum | solution.py:65
  112.8 1.0 multiply_reduce_fusion
  113.7 0.9 divide_convert_fusion
  114.7 0.5 fusion.26
  117.6 683.5 %scatter_custom_fusion = f32[262144]{0:T(1024)S(1)} fusion(s32[131072]{0:T(1024)} %bitcast.95, f32[131072]{0:T(1024)S(1)} %add_add_fusion, f32[]{:T(128)} %constant.69.clone.1), kind=kCustom, calls=%fused_computation.24 | custom fusion | flops 131072 | bytes 1049088 | tf_op jit(solution)/shard_map/scatter-add | solution.py:81
  801.1 0.4 reshape.123
  801.5 0.8 copy.26
  802.4 1.1 copy.20
  803.5 52.0 %all-reduce.5.cloned.1.call-done = f32[262144]{0:T(1024)} async-done(((f32[262144]{0:T(1024)}), f32[262144]{0:T(1024)}) %all-reduce.5.cloned.1.call-update) | async-done | bytes 1048592 | tf_op jit(solution)/shard_map/psum | solution.py:85
  855.5 1.0 dynamic_slice.14
  856.6 1.3 collective-permute-done
  857.9 1.0 fusion.20
  858.9 6.6 fusion.1
  865.6 40.0 %psum.23 = f32[3,128]{1,0:T(4,128)S(1)} all-reduce(f32[3,128]{1,0:T(4,128)S(1)} %fusion.1), channel_id=1, replica_groups=mesh['half'=2,'cls'=4,'vol'=4] {'half','cls','vol'}, use_global_device_ids=true, to_apply=%region_8.9 | all-reduce | flops 384 | bytes 3072 | tf_op jit(solution)/shard_map/psum | solution.py:98
  905.6 0.7 slice_reduce_fusion.2
  908.2 11.8 %fusion = f32[1,32768]{1,0:T(1,128)S(1)} fusion(s32[32768]{0:T(1024)S(1)} %bitcast.108, f32[1,128]{1,0:T(1,128)S(1)} %get-tuple-element.24), kind=kOutput, calls=%fused_computation.3 | convolution fusion | flops 54525952 | bytes 262656 | tf_op jit(solution)/shard_map/dot_general | solution.py:103
  920.0 0.7 multiply_divide_fusion
  (45 shorter events, 4.4 us)
Async XLA Ops:
  7.2 3.0 copy-start
  13.7 6.5 copy-start.1
  13.7 54.6 %all-to-all-start = ((bf16[4,64,4096]{2,1,0:T(8,128)(2,1)}), bf16[4,64,4096]{2,1,0:T(8,128)(2,1)S(1)}, u32[]{:S(2)}, u32[]{:S(2)}) async-start(bf16[4,64,4096]{2,1,0:T(8,128)(2,1)} %select_select_fusion), calls=%async_computation | async-start | bytes 4194304 | tf_op jit(solution)/shard_map/all_to_all | solution.py:42
  20.1 92.6 %all-reduce.3.cloned.1.call-start = ((), (), s32[]{:S(2)}) async-start(), calls=%async_computation.1 | async-start | bytes 327680 | tf_op jit(solution)/shard_map/psum | solution.py:65
  71.2 784.3 %all-reduce.5.cloned.1.call-start = ((), (), s32[]{:S(2)}) async-start(), calls=%async_computation.2 | async-start | bytes 2097152 | tf_op jit(solution)/shard_map/psum | solution.py:85
  802.4 56.6 %copy-start.3 = (s32[1,32768]{1,0:T(1,128)S(1)}, s32[1,32768]{1,0:T(1,128)}, u32[]{:S(2)}) copy-start(s32[1,32768]{1,0:T(1,128)} %param.9) | copy-start | bytes 393220
  856.5 1.4 collective-permute-start
  906.3 13.7 %copy-start.2 = (f32[1,128]{1,0:T(1,128)}, f32[1,128]{1,0:T(1,128)S(1)}, u32[]{:S(2)}) copy-start(f32[1,128]{1,0:T(1,128)S(1)} %get-tuple-element.24) | copy-start | bytes 1540
Sparse Core Ops, SparseCore 0:
  71.3 41.4 all-reduce.2
  803.6 51.8 all-reduce.4
where the time goes:
time: 928 us
  other arithmetic  695 us (75%)
  waiting for transfers between devices  136 us (15%)
  blocking collectives  40 us (4%)
  matrix products  21.8 us (2%)
  between operations  16.3 us (2%)
  local copies, waits for them, and re-layouts  12.3 us (1%)
    scatter-add x1, other arithmetic, shards(): jax.ops.segment_sum(aligned.reshape(-1), placed.reshape(-1), num_segments...  683 us
    psum x1, waiting for transfers between devices, shards(): slab_full = lax.psum(slab_part, 'cls')  52 us
    all_to_all x1, waiting for transfers between devices, shards(): lax.all_to_all(outgoing.reshape(n_cls, capacity, pix_quarter), 'cls', spl...  43 us
    psum x1, blocking collectives, shards(): shell_sums = lax.psum(shell_terms, ('half', 'cls', 'vol'))  40 us
    psum x1, waiting for transfers between devices, shards(): scores = lax.psum(partial_scores, 'vol')  39.5 us
  transfers between devices with their start and end apart: 4, of which 4 were waited for; matrix products, arithmetic and copies ran while one was open for 1% of the time, Pallas kernels for 0%

commit v1 on v0

--- a/solution.py
+++ b/solution.py
@@ -1,6 +1,10 @@
+import functools
+
 import jax
 import jax.numpy as jnp
 from jax import lax
+from jax.experimental import pallas as pl
+from jax.experimental.pallas import tpu as pltpu
 from jax.sharding import PartitionSpec as P
 
 IMG = 128
@@ -19,17 +23,396 @@
     return lax.ppermute(shard, axis, [(i, i ^ 1 << apart) for i in range(lax.axis_size(axis))])
 
 
+def insert_body(place_ref, value_ref, out_ref):
+    cols, count = place_ref.shape
+    chunk = min(count, 1024)
+    low_ids = lax.broadcasted_iota(jnp.int32, (128, chunk), 0)
+    high_ids = lax.broadcasted_iota(jnp.int32, (16, chunk), 0)
+    for col in range(cols):
+        total = jnp.zeros((32, 128), jnp.float32)
+        for start in range(0, count, chunk):
+            place = place_ref[col : col + 1, start : start + chunk]
+            value = value_ref[col : col + 1, start : start + chunk]
+            coarse = value.astype(jnp.bfloat16).astype(jnp.float32)
+            fine = value - coarse
+            hit = high_ids == (place >> 7)
+            left = jnp.concatenate(
+                [jnp.where(hit, coarse, 0.0), jnp.where(hit, fine, 0.0)], axis=0
+            ).astype(jnp.bfloat16)
+            right = jnp.where(low_ids == (place & 127), 1.0, 0.0).astype(jnp.bfloat16)
+            total += lax.dot_general(
+                left, right, (((1,), (1,)), ((), ())), preferred_element_type=jnp.float32
+            )
+        out_ref[col] = total[:16] + total[16:]
+
+
+def insert(place, value):
+    cols, count = place.shape
+    step = 8
+    return pl.pallas_call(
+        insert_body,
+        grid=(cols // step,),
+        in_specs=[pl.BlockSpec((step, count), lambda i: (i, 0))] * 2,
+        out_specs=pl.BlockSpec((step, 16, 128), lambda i: (i, 0, 0)),
+        out_shape=jax.ShapeDtypeStruct((cols, 16, 128), jnp.float32),
+        compiler_params=pltpu.CompilerParams(vmem_limit_bytes=32 << 20),
+    )(place, value)
+
+
+def fused_body(
+    n_cls, n_vol, images, refs, places, groups, shells, volume, fsc_out,
+    rolled, refs_all, places_all, places32, scores, score_box, flipped, by_col, by_col_in,
+    slab, slab_in, hot, stat_half, stat_cls, stat_vol,
+    ref_send, ref_recv, fwd_send, fwd_recv, place_send, place_recv, score_send, score_recv,
+    half_send, half_recv, slab_send, slab_recv, stat_send, stat_recv,
+):
+    half, cls, vol = lax.axis_index("half"), lax.axis_index("cls"), lax.axis_index("vol")
+    other = 1 - half
+    part_count, pix = images.shape
+    class_count = refs.shape[0]
+    split = class_count // 2
+    cols = IMG // 2
+    own_cols = cols // n_cls
+    mine = (half, cls, vol)
+
+    def along(axis, step):
+        at = list(mine)
+        at[axis] = lax.rem(mine[axis] + step, (2, n_cls, n_vol)[axis])
+        return tuple(at)
+
+    def push(src, dst, send, recv, target):
+        return pltpu.make_async_remote_copy(
+            src_ref=src, dst_ref=dst, send_sem=send, recv_sem=recv,
+            device_id=target, device_id_type=pl.DeviceIdType.MESH,
+        )
+
+    peers = [along(0, 1)]
+    peers += [along(1, t) for t in range(1, n_cls)] + [along(2, t) for t in range(1, n_vol)]
+    barrier = pltpu.get_barrier_semaphore()
+    for peer in peers:
+        pl.semaphore_signal(barrier, inc=1, device_id=peer, device_id_type=pl.DeviceIdType.MESH)
+    pl.semaphore_wait(barrier, len(peers))
+
+    ref_copies, place_copies, fwd_copies = [], [], []
+    for t in range(1, n_cls):
+        ref_copies.append(push(
+            refs.at[pl.ds(half * split, split)],
+            refs_all.at[pl.ds(cls * class_count + half * split, split)],
+            ref_send.at[t - 1], ref_recv.at[t - 1], along(1, t),
+        ))
+        ref_copies[-1].start()
+    for t in range(1, n_cls):
+        place_copies.append(push(
+            places.at[pl.ds(half * cols, cols)], places_all.at[cls],
+            place_send.at[t - 1], place_recv.at[t - 1], along(1, t),
+        ))
+        place_copies[-1].start()
+    refs_all[pl.ds(cls * class_count, class_count), :] = refs[...]
+
+    def roll_rows(r, carry):
+        at = pl.ds(pl.multiple_of(r * IMG, IMG), IMG)
+        band = images[:, at].astype(jnp.float32)
+        for i in range(SHIFTS):
+            turned = pltpu.roll(band, (i - SHIFTS // 2) % IMG, 1)
+            rolled[i * part_count : (i + 1) * part_count, at] = turned.astype(jnp.bfloat16)
+        return carry
+
+    lax.fori_loop(0, pix // IMG, roll_rows, 0)
+
+    for t in range(1, n_cls):
+        ref_copies[t - 1].wait_recv()
+        source = lax.rem(cls - t + n_cls, n_cls)
+        rows = pl.ds(source * class_count + half * split, split)
+        fwd_copies.append(push(
+            refs_all.at[rows], refs_all.at[rows], fwd_send.at[t - 1], fwd_recv.at[t - 1], along(0, 1)
+        ))
+        fwd_copies[-1].start()
+    for copy in fwd_copies:
+        copy.wait_recv()
+
+    scores[...] = jnp.zeros_like(scores)
+
+    def score_step(m, carry):
+        at = pl.ds(pl.multiple_of(m * 512, 512), 512)
+        scores[...] += lax.dot_general(
+            rolled[:, at], refs_all[:, at], (((1,), (1,)), ((), ())),
+            preferred_element_type=jnp.float32,
+        )
+        return carry
+
+    lax.fori_loop(0, pix // 512, score_step, 0)
+
+    lanes = 4 * class_count
+    lane_block = lax.broadcasted_iota(jnp.int32, (part_count, lanes), 1) // class_count
+    own_group = groups[...] == lane_block
+
+    def spread(x):
+        x = x + pltpu.roll(x, lanes // 2, 1)
+        return x + pltpu.roll(x, lanes // 4, 1)
+
+    packed = jnp.zeros((part_count, lanes), jnp.float32)
+    for i in range(4):
+        part = jnp.where(own_group, scores[i * part_count : (i + 1) * part_count, :], 0.0)
+        packed = jnp.where(lane_block == i, spread(part), packed)
+    last = spread(jnp.where(own_group, scores[4 * part_count :, :], 0.0))
+    quarter = part_count // 4
+    tail = jnp.zeros((quarter, lanes), jnp.float32)
+    for b in range(4):
+        tail = jnp.where(lane_block[:quarter] == b, last[b * quarter : (b + 1) * quarter], tail)
+    score_box[vol, 0:part_count, :] = packed
+    score_box[vol, part_count : part_count + quarter, :] = tail
+    score_copies = []
+    for t in range(1, n_vol):
+        score_copies.append(push(
+            score_box.at[vol], score_box.at[vol], score_send.at[t - 1], score_recv.at[t - 1], along(2, t)
+        ))
+        score_copies[-1].start()
+    for copy in score_copies:
+        copy.wait()
+    summed = score_box[0]
+    for v in range(1, n_vol):
+        summed = summed + score_box[v]
+    packed, tail = summed[:part_count], summed[part_count:]
+    squares = []
+    for i in range(4):
+        part = spread(jnp.where(lane_block == i, packed, 0.0))
+        squares.append(part * part)
+    last = jnp.concatenate(
+        [spread(jnp.where(lane_block[:quarter] == b, tail, 0.0)) for b in range(4)], axis=0
+    )
+    squares.append(last * last)
+    total = squares[0]
+    for i in range(1, SHIFTS):
+        total = total + squares[i]
+    mean_square = jnp.sum(total, axis=1, keepdims=True) * (1.0 / (4 * SHIFTS * class_count))
+    for i in range(SHIFTS):
+        weight = jnp.where(own_group, squares[i] / (mean_square + EPS_W), 0.0)
+        flipped[:, i * part_count : (i + 1) * part_count] = weight.T.astype(jnp.bfloat16)
+
+    tiles = pix // IMG // 4
+
+    def sum_step(m, carry):
+        block = lax.dot_general(
+            flipped[...], rolled[:, pl.ds(pl.multiple_of(m * 4 * IMG, 4 * IMG), 4 * IMG)],
+            (((1,), (0,)), ((), ())), preferred_element_type=jnp.float32,
+        )
+        for g in range(n_cls):
+            tile = jnp.concatenate(
+                [
+                    block[g * class_count : (g + 1) * class_count, r * IMG : (r + 1) * IMG]
+                    for r in range(4)
+                ],
+                axis=0,
+            )
+            at = pl.ds(pl.multiple_of((g * tiles + m) * IMG, IMG), IMG)
+            by_col[:, at] = tile.T
+        return carry
+
+    lax.fori_loop(0, tiles, sum_step, 0)
+    half_copy = push(
+        by_col.at[pl.ds(other * cols, cols)], by_col_in, half_send.at[0], half_recv.at[0], along(0, 1)
+    )
+    half_copy.start()
+    for copy in place_copies:
+        copy.wait_recv()
+    places32[cls] = places[pl.ds(pl.multiple_of(half * cols, cols), cols), :].astype(jnp.int32)
+    for t in range(1, n_cls):
+        source = lax.rem(cls - t + n_cls, n_cls)
+        places32[source] = places_all[source].astype(jnp.int32)
+    half_copy.wait()
+
+    chunk = places.shape[1]
+    low_ids = lax.broadcasted_iota(jnp.int32, (128, chunk), 0)
+    high_ids = lax.broadcasted_iota(jnp.int32, (16, chunk), 0)
+
+    def insert_eight(target, eight):
+        base = pl.multiple_of(target * own_cols + eight * 8, 8)
+        for j in range(8):
+            total = jnp.zeros((64, 128), jnp.float32)
+            for g in range(n_cls):
+                span = slice(g * chunk, (g + 1) * chunk)
+                place = places32[g, pl.ds(base, 8), :][j : j + 1]
+                own = by_col[pl.ds(pl.multiple_of(half * cols + base, 8), 8), span][j : j + 1]
+                got = by_col_in[pl.ds(base, 8), span][j : j + 1]
+                hit = high_ids == (place >> 7)
+                parts = []
+                for value in (own, got):
+                    coarse = value.astype(jnp.bfloat16).astype(jnp.float32)
+                    fine = value - coarse
+                    parts += [jnp.where(hit, coarse, 0.0), jnp.where(hit, fine, 0.0)]
+                left = jnp.concatenate(parts, axis=0).astype(jnp.bfloat16)
+                right = jnp.where(low_ids == (place & 127), 1.0, 0.0).astype(jnp.bfloat16)
+                total += lax.dot_general(
+                    left, right, (((1,), (1,)), ((), ())), preferred_element_type=jnp.float32
+                )
+            rows = pl.ds(pl.multiple_of(eight * 128 + j * 16, 16), 16)
+            slab[target, 0, rows, :] = total[0:16] + total[16:32]
+            slab[target, 1, rows, :] = total[32:48] + total[48:64]
+
+    slab_copies = []
+    for t in range(1, n_cls + 1):
+        target = lax.rem(cls + t, n_cls)
+
+        def eight_step(e, carry, target=target):
+            insert_eight(target, e)
+            return carry
+
+        lax.fori_loop(0, own_cols // 8, eight_step, 0)
+        if t < n_cls:
+            slab_copies.append(push(
+                slab.at[target], slab_in.at[t - 1], slab_send.at[t - 1], slab_recv.at[t - 1], along(1, t)
+            ))
+            slab_copies[-1].start()
+    for copy in slab_copies:
+        copy.wait()
+
+    shell_ids = lax.broadcasted_iota(jnp.int32, (NSHELL, 128), 0)
+    blank = jnp.zeros((1, 128), jnp.float32)
+
+    def stat_step(m, carry):
+        rows = pl.ds(pl.multiple_of(m * 8, 8), 8)
+        maps = []
+        for k in range(2):
+            x = slab[cls, k, rows, :]
+            for t in range(1, n_cls):
+                x = x + slab_in[t - 1, k, rows, :]
+            maps.append(x)
+            slab[cls, k, rows, :] = x
+        terms = []
+        for x in (maps[0] * maps[0], maps[1] * maps[1], maps[0] * maps[1]):
+            coarse = x.astype(jnp.bfloat16).astype(jnp.float32)
+            terms += [coarse, x - coarse]
+        shell = shells[rows, :]
+        left = jnp.concatenate(
+            [
+                jnp.concatenate([x[j : j + 1] for x in terms] + [blank, blank], axis=0)
+                for j in range(8)
+            ],
+            axis=1,
+        ).astype(jnp.bfloat16)
+        right = jnp.concatenate(
+            [
+                jnp.where(shell_ids == shell[j : j + 1], 1.0, 0.0).astype(jnp.bfloat16)
+                for j in range(8)
+            ],
+            axis=1,
+        )
+        hot[m] = right
+        return carry + lax.dot_general(
+            left, right, (((1,), (1,)), ((), ())), preferred_element_type=jnp.float32
+        )
+
+    blocks = shells.shape[0] // 8
+    sums = lax.fori_loop(0, blocks, stat_step, jnp.zeros((8, NSHELL), jnp.float32))
+    mine_sq, other_sq, cross = sums[0:1] + sums[1:2], sums[2:3] + sums[3:4], sums[4:5] + sums[5:6]
+    row_ids = lax.broadcasted_iota(jnp.int32, (8, NSHELL), 0)
+    swap = jnp.full((1, NSHELL), half, jnp.int32) == 1
+    first_sq = jnp.where(swap, other_sq, mine_sq)
+    second_sq = jnp.where(swap, mine_sq, other_sq)
+    stat = jnp.where(row_ids == 0, first_sq, jnp.where(row_ids == 1, second_sq, cross))
+    at = 0
+    for axis, box in enumerate((stat_half, stat_cls, stat_vol)):
+        size = box.shape[0]
+        box[mine[axis]] = stat
+        copies = []
+        for t in range(1, size):
+            copies.append(push(
+                box.at[mine[axis]], box.at[mine[axis]], stat_send.at[at], stat_recv.at[at], along(axis, t)
+            ))
+            copies[-1].start()
+            at += 1
+        for copy in copies:
+            copy.wait()
+        stat = box[0]
+        for k in range(1, size):
+            stat = stat + box[k]
+    first_sq, second_sq, cross = stat[0:1], stat[1:2], stat[2:3]
+    fsc = cross / (jnp.sqrt(first_sq) * jnp.sqrt(second_sq) + EPS_F)
+    fsc_out[...] = fsc
+    mean_sq = jnp.sum(first_sq + second_sq + 2.0 * cross, axis=1, keepdims=True) * (
+        1.0 / (4.0 * n_vol * VOXS)
+    )
+    scale = 0.5 / jnp.sqrt(mean_sq + EPS_F)
+    coarse = fsc.astype(jnp.bfloat16).astype(jnp.float32)
+    pair = jnp.where(row_ids == 0, coarse, jnp.where(row_ids == 1, fsc - coarse, 0.0)).astype(jnp.bfloat16)
+
+    def volume_step(m, carry):
+        rows = pl.ds(pl.multiple_of(m * 8, 8), 8)
+        picked = jnp.dot(pair, hot[m], preferred_element_type=jnp.float32)
+        picked = picked[0:1] + picked[1:2]
+        weight = jnp.concatenate([picked[:, j * 128 : (j + 1) * 128] for j in range(8)], axis=0)
+        volume[rows, :] = weight * (slab[cls, 0, rows, :] + slab[cls, 1, rows, :]) * scale
+        return carry
+
+    lax.fori_loop(0, blocks, volume_step, 0)
+    for copy in ref_copies + place_copies + fwd_copies:
+        copy.wait_send()
+
+
+def fused(images, groups, references, interp_index, shell_index):
+    n_cls, n_vol = lax.axis_size("cls"), lax.axis_size("vol")
+    part_count, pix = images.shape
+    class_count = references.shape[0]
+    rows = pix // IMG
+    piece = shell_index.shape[1] // 128
+    places = jnp.transpose(interp_index.astype(jnp.int16).reshape(class_count, rows, IMG), (2, 1, 0))
+    places = places.reshape(IMG, rows * class_count)
+    lanes = n_cls * class_count
+    count = rows * class_count
+    half_cols = IMG // 2
+    dma = pltpu.SemaphoreType.DMA
+    bf16, f32 = jnp.bfloat16, jnp.float32
+    volume, fsc = pl.pallas_call(
+        functools.partial(fused_body, n_cls, n_vol),
+        out_shape=(
+            jax.ShapeDtypeStruct((piece, 128), f32),
+            jax.ShapeDtypeStruct((1, NSHELL), f32),
+        ),
+        in_specs=[pl.BlockSpec(memory_space=pltpu.VMEM)] * 5,
+        out_specs=(pl.BlockSpec(memory_space=pltpu.VMEM),) * 2,
+        scratch_shapes=[
+            pltpu.VMEM((SHIFTS * part_count, pix), bf16),
+            pltpu.VMEM((lanes, pix), bf16),
+            pltpu.VMEM((n_cls, half_cols, count), jnp.int16),
+            pltpu.VMEM((n_cls, half_cols, count), jnp.int32),
+            pltpu.VMEM((SHIFTS * part_count, lanes), f32),
+            pltpu.VMEM((n_vol, part_count + part_count // 4, lanes), f32),
+            pltpu.VMEM((lanes, SHIFTS * part_count), bf16),
+            pltpu.VMEM((IMG, n_cls * count), f32),
+            pltpu.VMEM((half_cols, n_cls * count), f32),
+            pltpu.VMEM((n_cls, 2, piece, 128), f32),
+            pltpu.VMEM((n_cls - 1, 2, piece, 128), f32),
+            pltpu.VMEM((piece // 8, NSHELL, 1024), bf16),
+            pltpu.VMEM((2, 8, NSHELL), f32),
+            pltpu.VMEM((n_cls, 8, NSHELL), f32),
+            pltpu.VMEM((n_vol, 8, NSHELL), f32),
+        ]
+        + [dma((n_cls - 1,))] * 6
+        + [dma((n_vol - 1,))] * 2
+        + [dma((1,))] * 2
+        + [dma((n_cls - 1,))] * 2
+        + [dma((n_cls + n_vol - 1,))] * 2,
+        compiler_params=pltpu.CompilerParams(
+            collective_id=0, has_side_effects=True, vmem_limit_bytes=56 << 20
+        ),
+    )(images, references, places, groups, shell_index.reshape(piece, 128))
+    return (volume.reshape(1, -1), fsc[0])
+
+
 def shards(images, groups, references, interp_index, shell_index):
     n_cls = lax.axis_size("cls")
     n_vol = lax.axis_size("vol")
     n_half = lax.axis_size("half")
     part_count, pix_quarter = images.shape
     class_count = references.shape[0]
+    if n_half == 2 and n_cls == 4 and class_count == 32:
+        return fused(images, groups, references, interp_index, shell_index)
     capacity = max(2 * part_count // n_cls, 4)
     slot_count = n_cls * capacity
     owner_ids = groups[:, 0]
-    matches = (owner_ids[:, None] == jnp.arange(n_cls, dtype=jnp.int32)[None, :]).astype(jnp.int32)
-    order_in = jnp.sum(jnp.cumsum(matches, axis=0) * matches, axis=1) - 1
+    same = owner_ids[:, None] == owner_ids[None, :]
+    earlier = jnp.arange(part_count)[None, :] < jnp.arange(part_count)[:, None]
+    order_in = jnp.sum((same & earlier).astype(jnp.int32), axis=1)
     slot_ids = owner_ids * capacity + order_in
     slot_hits = slot_ids[None, :] == jnp.arange(slot_count, dtype=jnp.int32)[:, None]
     source_ids = jnp.sum(
@@ -76,9 +459,8 @@
     aligned = jnp.roll(weighted[0], -(SHIFTS // 2), axis=2)
     for shift_id in range(1, SHIFTS):
         aligned = aligned + jnp.roll(weighted[shift_id], shift_id - SHIFTS // 2, axis=2)
-    column_ids = jnp.arange(pix_quarter, dtype=jnp.int32) % IMG
-    placed = interp_index + 2 * VBOX * PLANES * column_ids[None, :]
-    slab_part = jax.ops.segment_sum(aligned.reshape(-1), placed.reshape(-1), num_segments=VOXS)
+    by_column = jnp.transpose(interp_index.reshape(-1, IMG))
+    slab_part = insert(by_column, jnp.transpose(aligned.reshape(-1, IMG)))
     piece_len = VOXS // (n_half * n_cls)
     slab_part = jnp.transpose(slab_part.reshape(n_half, n_cls, piece_len), (1, 0, 2)).reshape(-1)
     block_len = VOXS // n_cls

time: 928 us -> 97.4 us (0.10)
  other arithmetic: 695 us -> 1.08 us
  waiting for transfers between devices: 136 us -> 0 us
  Pallas kernels: 0 us -> 91.6 us
  blocking collectives: 40 us -> 0 us
  matrix products: 21.8 us -> 0 us
  between operations: 16.3 us -> 0.67 us
    scatter-add x1 -> x0, other arithmetic: 683 us -> none  [shards(): jax.ops.segment_sum(aligned.reshape(-1), placed.reshape(-1), num_segments...]
    pallas_call x0 -> x1, Pallas kernels: none -> 91.6 us  [fused(): pl.pallas_call(functools.partial(fused_body, n_cls, n_vol), out_shape=(ja...]
    psum x2 -> x0, waiting for transfers between devices: 91.5 us -> none  [the longest x1 52 us: shards(): slab_full = lax.psum(slab_part, 'cls')]
    all_to_all x1 -> x0, waiting for transfers between devices: 43 us -> none  [shards(): lax.all_to_all(outgoing.reshape(n_cls, capacity, pix_quarter), 'cls', spl...]
    psum x1 -> x0, blocking collectives: 40 us -> none  [shards(): shell_sums = lax.psum(shell_terms, ('half', 'cls', 'vol'))]
    dot_general x4 -> x0, matrix products: 21.8 us -> none  [the longest x1 11.8 us: shards(): filter_vox = jnp.dot(shell_hot, shell_fsc, precision=lax.Precision.HIGHEST)]
  transfers between devices with their start and end apart: 4 -> 0, of which waited for: 4 -> 0; matrix products, arithmetic and copies ran while one was open for 1% -> 0% of each run, Pallas kernels for 0% -> 0%
where the time goes in v1:
time: 97.4 us; the launch traced here: 97.2 us
  Pallas kernels  91.6 us (94%)
  local copies, waits for them, and re-layouts  3.88 us (4%)
  other arithmetic  1.08 us (1%)
    pallas_call x1, Pallas kernels, fused(): pl.pallas_call(functools.partial(fused_body, n_cls, n_vol), out_shape=(ja...  91.6 us
    unnamed x8, local copies, waits for them, and re-layouts  2.87 us

profile of v1, /device:TPU:0, one launch (start us, length us, event | category | flops | bytes accessed | tf_op | source)
XLA Modules:
  0.0 97.2 jit_solution(10878921284537798015)
XLA Ops:
  0.6 1.1 %convert_bitcast_fusion = s16[4,8,32,128]{3,1,2,0:T(8,128)(2,1)S(1)} fusion(s32[32,4096]{1,0:T(8,128)} %param.8), kind=kLoop, calls=%fused_computation | loop fusion | flops 131072 | bytes 786432
  1.8 0.1 copy.11
  1.9 0.0 copy-start
  1.9 0.9 copy.12.places
  2.8 0.0 copy-done
  2.8 0.7 copy.13.groups
  3.5 91.6 %shard_map.68 = (f32[256,128]{1,0:T(8,128)}, f32[1,128]{1,0:T(1,128)}) custom-call(bf16[128,4096]{1,0:T(8,128)(2,1)} %images.1, bf16[32,4096]{1,0:T(8,128)(2,1)} %refs.1, s16[128,1024]{1,0:T(8,128)(2,1)} %copy.12.places, s32[128,1]{1,0:T(8,128)} %copy.13.groups, s32[256,128]{1,0:T(8,128)} %bitcast.11), custom_call_target="tpu_custom_call" | custom-call | tf_op jit(solution)/shard_map/pallas_call | solution.py:365
  95.1 0.0 copy-start.1
  95.1 1.6 %copy.17 = f32[1,32768]{1,0:T(1,128)} copy(f32[1,32768]{1,0:T(1,128)} %bitcast.12) | data formatting | bytes 262144
  96.7 0.0 copy-done.1
  96.7 0.5 copy.18
  (1 shorter events, 0.0 us)
Async XLA Ops:
  1.9 0.9 copy-start
  95.1 1.6 %copy-start.1 = (f32[1,128]{1,0:T(1,128)S(1)}, f32[1,128]{1,0:T(1,128)}, u32[]{:S(2)}) copy-start(f32[1,128]{1,0:T(1,128)} %get-tuple-element.5) | copy-start | bytes 1540

commit v2 on v1

--- a/solution.py
+++ b/solution.py
@@ -101,12 +101,6 @@
             ref_send.at[t - 1], ref_recv.at[t - 1], along(1, t),
         ))
         ref_copies[-1].start()
-    for t in range(1, n_cls):
-        place_copies.append(push(
-            places.at[pl.ds(half * cols, cols)], places_all.at[cls],
-            place_send.at[t - 1], place_recv.at[t - 1], along(1, t),
-        ))
-        place_copies[-1].start()
     refs_all[pl.ds(cls * class_count, class_count), :] = refs[...]
 
     def roll_rows(r, carry):
@@ -127,6 +121,12 @@
             refs_all.at[rows], refs_all.at[rows], fwd_send.at[t - 1], fwd_recv.at[t - 1], along(0, 1)
         ))
         fwd_copies[-1].start()
+    for t in range(1, n_cls):
+        place_copies.append(push(
+            places.at[pl.ds(half * cols, cols)], places_all.at[cls],
+            place_send.at[t - 1], place_recv.at[t - 1], along(1, t),
+        ))
+        place_copies[-1].start()
     for copy in fwd_copies:
         copy.wait_recv()
 
@@ -208,7 +208,7 @@
             by_col[:, at] = tile.T
         return carry
 
-    lax.fori_loop(0, tiles, sum_step, 0)
+    lax.fori_loop(0, tiles, sum_step, 0, unroll=2)
     half_copy = push(
         by_col.at[pl.ds(other * cols, cols)], by_col_in, half_send.at[0], half_recv.at[0], along(0, 1)
     )
@@ -303,7 +303,7 @@
         )
 
     blocks = shells.shape[0] // 8
-    sums = lax.fori_loop(0, blocks, stat_step, jnp.zeros((8, NSHELL), jnp.float32))
+    sums = lax.fori_loop(0, blocks, stat_step, jnp.zeros((8, NSHELL), jnp.float32), unroll=4)
     mine_sq, other_sq, cross = sums[0:1] + sums[1:2], sums[2:3] + sums[3:4], sums[4:5] + sums[5:6]
     row_ids = lax.broadcasted_iota(jnp.int32, (8, NSHELL), 0)
     swap = jnp.full((1, NSHELL), half, jnp.int32) == 1
@@ -344,7 +344,7 @@
         volume[rows, :] = weight * (slab[cls, 0, rows, :] + slab[cls, 1, rows, :]) * scale
         return carry
 
-    lax.fori_loop(0, blocks, volume_step, 0)
+    lax.fori_loop(0, blocks, volume_step, 0, unroll=4)
     for copy in ref_copies + place_copies + fwd_copies:
         copy.wait_send()
 

time: 97.4 us -> 85.6 us (0.88)
  Pallas kernels: 91.6 us -> 79.8 us
    pallas_call x1, Pallas kernels: 91.6 us -> 79.8 us  [fused(): pl.pallas_call(functools.partial(fused_body, n_cls, n_vol), out_shape=(ja...]
where the time goes in v2:
time: 85.6 us; the launch traced here: 85.4 us
  Pallas kernels  79.8 us (93%)
  local copies, waits for them, and re-layouts  3.88 us (5%)
  other arithmetic  1.08 us (1%)
    pallas_call x1, Pallas kernels, fused(): pl.pallas_call(functools.partial(fused_body, n_cls, n_vol), out_shape=(ja...  79.8 us
    unnamed x8, local copies, waits for them, and re-layouts  2.87 us

profile of v2, /device:TPU:0, one launch (start us, length us, event | category | flops | bytes accessed | tf_op | source)
XLA Modules:
  0.0 85.4 jit_solution(11456633724653952840)
XLA Ops:
  0.6 1.1 %convert_bitcast_fusion = s16[4,8,32,128]{3,1,2,0:T(8,128)(2,1)S(1)} fusion(s32[32,4096]{1,0:T(8,128)} %param.8), kind=kLoop, calls=%fused_computation | loop fusion | flops 131072 | bytes 786432
  1.8 0.1 copy.11
  1.9 0.0 copy-start
  1.9 0.9 %copy.12.places = s16[128,1024]{1,0:T(8,128)(2,1)} copy(s16[128,1024]{0,1:T(8,128)(2,1)S(1)} %bitcast.10) | data formatting | bytes 524288 | tf_op jit(solution)/shard_map/reshape | solution.py:359
  2.8 0.0 copy-done
  2.8 0.7 copy.13.groups
  3.5 79.8 %shard_map.68 = (f32[256,128]{1,0:T(8,128)}, f32[1,128]{1,0:T(1,128)}) custom-call(bf16[128,4096]{1,0:T(8,128)(2,1)} %images.1, bf16[32,4096]{1,0:T(8,128)(2,1)} %refs.1, s16[128,1024]{1,0:T(8,128)(2,1)} %copy.12.places, s32[128,1]{1,0:T(8,128)} %copy.13.groups, s32[256,128]{1,0:T(8,128)} %bitcast.11), custom_call_target="tpu_custom_call" | custom-call | tf_op jit(solution)/shard_map/pallas_call | solution.py:365
  83.3 0.0 copy-start.1
  83.3 1.6 %copy.17 = f32[1,32768]{1,0:T(1,128)} copy(f32[1,32768]{1,0:T(1,128)} %bitcast.12) | data formatting | bytes 262144
  84.9 0.0 copy-done.1
  84.9 0.5 copy.18
  (1 shorter events, 0.0 us)
Async XLA Ops:
  1.9 0.9 %copy-start = (s32[128,1]{0,1:T(1,128)S(1)}, s32[128,1]{0,1:T(1,128)}, u32[]{:S(2)}) copy-start(s32[128,1]{0,1:T(1,128)} %param.6) | copy-start | bytes 1540
  83.3 1.6 %copy-start.1 = (f32[1,128]{1,0:T(1,128)S(1)}, f32[1,128]{1,0:T(1,128)}, u32[]{:S(2)}) copy-start(f32[1,128]{1,0:T(1,128)} %get-tuple-element.5) | copy-start | bytes 1540
